TPU v7x, 128 devices: a whole 4x4x4 slice. The times are simulated.
128 devices in a mesh: prow: 8 (over x_lo, z), pcol: 16 (over x_hi, y, core).
Axes of the slice: x: 4 (x_hi: 2, x_lo: 2; x = x_hi * 2 + x_lo), y: 4, z: 4, core: 2. Of those that a mesh axis runs over, the one named last changes fastest.
Arguments:
- k_star: float32 [4, 16, 512, 256], P(None, 'pcol', 'prow'), may hold values from -6 to 6
- lower_blocks: float32 [6, 16, 512, 8192], P(None, None, 'prow', 'pcol'), may hold values from -0.046875 to 0.046875
- diag_inverse: float32 [4, 16, 512, 8192], P(None, None, 'prow', 'pcol'), may hold values from -1 to 2, as said below
Outputs:
- forward_solution: float32 [4, 16, 512, 256], P(None, 'pcol', 'prow')
- solution: float32 [4, 16, 512, 256], P(None, 'pcol', 'prow')
Inputs may be any that keep to these rules, and one draw needn't show every extreme that they name: Each of the 4 blocks of diag_inverse is lower triangular with a positive diagonal.
All inputs are finite; a program needn't handle non-finite values.
Results may differ from a plain program's by a relative error of at most 0.00013.
Values sent between devices are 32-bit elements; how exact they have to be, the bound alone decides.
A program may use at most 128 MiB of HBM per device.

v0:
```python
import jax
import jax.numpy as jnp
from jax import lax
from jax.sharding import PartitionSpec as P


def product(left, right):
    return jnp.dot(left, right, precision=lax.Precision.HIGHEST, preferred_element_type=jnp.float32)


def product_left(left, right):
    return lax.dot_general(
        left,
        right,
        (((0,), (0,)), ((), ())),
        precision=lax.Precision.HIGHEST,
        preferred_element_type=jnp.float32,
    )


def pair_index(row_block, col_block):
    return row_block * (row_block - 1) // 2 + col_block


def sum_columns(term, piece):
    return lax.psum_scatter(
        term(jnp.int32(0), piece * lax.axis_size("pcol")), "pcol", scatter_dimension=0, tiled=True
    )


def sum_rows(term, piece):
    return lax.psum_scatter(
        term(jnp.int32(0), piece * lax.axis_size("prow")), "prow", scatter_dimension=0, tiled=True
    )


def slicer(values):

    def take(start, count):
        return values

    return take


def forward_update(lower, block, columns):

    def term(start, count):
        total = None
        for other in range(block):
            rows = lower[pair_index(block, other)]
            part_sum = product(rows, columns[other])
            total = part_sum if total is None else total + part_sum
        return total

    return term


def backward_update(lower, block, row_values, steps_count):

    def term(start, count):
        total = None
        for other in range(block + 1, steps_count):
            cols = lower[pair_index(other, block)]
            part_sum = product_left(cols, row_values[other])
            total = part_sum if total is None else total + part_sum
        return total

    return term


def apply_inverse(reduced, tile):

    def accumulate(carry, part, start):
        return product(tile, part)

    empty = jnp.zeros((tile.shape[0], reduced.shape[1]), jnp.float32)
    return accumulate(empty, lax.all_gather(reduced, "prow", axis=0, tiled=True), jnp.int32(0))


def apply_inverse_transposed(reduced, tile):

    def accumulate(carry, part, start):
        return product_left(tile, part)

    empty = jnp.zeros((tile.shape[1], reduced.shape[1]), jnp.float32)
    return accumulate(empty, lax.all_gather(reduced, "pcol", axis=0, tiled=True), jnp.int32(0))


def local(k_star, lower_blocks, diag_inverse):
    steps_count, _, piece, total_cols = k_star.shape
    pairs, col_groups, _, width = lower_blocks.shape
    lower = lower_blocks.reshape(pairs, col_groups * piece, width)
    inverse = diag_inverse.reshape(steps_count, col_groups * piece, width)
    bounds = [(0, total_cols)]
    panel_rhs = [k_star[:, 0, :, start:stop] for start, stop in bounds]
    forward_pieces = [[] for start, stop in bounds]
    forward_columns = [[] for start, stop in bounds]
    for block in range(steps_count):
        panel = 0
        reduced = panel_rhs[panel][block]
        if block > 0:
            reduced = reduced - sum_columns(
                forward_update(lower, block, forward_columns[panel]), piece
            )
        image = apply_inverse(reduced, inverse[block])
        solved = sum_columns(slicer(image), piece)
        forward_pieces[panel].append(solved)
        if block < steps_count - 1:
            forward_columns[panel].append(lax.all_gather(solved, "prow", axis=0, tiled=True))
    backward_pieces = [[None] * steps_count for start, stop in bounds]
    backward_rows = [[None] * steps_count for start, stop in bounds]
    for block in range(steps_count - 1, -1, -1):
        panel = 0
        reduced = forward_pieces[panel][block]
        if block < steps_count - 1:
            reduced = reduced - sum_rows(
                backward_update(lower, block, backward_rows[panel], steps_count), piece
            )
        image = apply_inverse_transposed(reduced, inverse[block])
        solved = sum_rows(slicer(image), piece)
        backward_pieces[panel][block] = solved
        if block > 0:
            backward_rows[panel][block] = lax.all_gather(solved, "pcol", axis=0, tiled=True)
    shape = (steps_count, 1, piece, total_cols)
    forward_out = jnp.concatenate([jnp.stack(pieces) for pieces in forward_pieces], axis=2).reshape(
        shape
    )
    backward_out = jnp.concatenate(
        [jnp.stack(pieces) for pieces in backward_pieces], axis=2
    ).reshape(shape)
    return (forward_out, backward_out)


def solution(mesh):
    return jax.shard_map(
        local,
        mesh=mesh,
        in_specs=(
            P(None, "pcol", "prow", None),
            P(None, None, "prow", "pcol"),
            P(None, None, "prow", "pcol"),
        ),
        out_specs=(P(None, "pcol", "prow", None), P(None, "pcol", "prow", None)),
        check_vma=False,
    )
```

profile of v0, /device:TPU:1, one launch (start us, length us, event | category | flops | bytes accessed | tf_op | source)
XLA Modules:
  0.0 1349.1 jit_solution(5761952054797772847)
XLA Ops:
  7.2 7.0 fusion.7
  14.2 25.4 %all-gather = f32[1,1,512,256]{3,2,1,0:T(8,128)S(1)} all-gather(f32[1,1,64,256]{3,2,1,0:T(8,128)S(1)} %slice-done), channel_id=2, replica_groups=mesh['prow'=8,'pcol'=16] {'prow'}, dimensions={2}, use_global_device_ids=true | all-gather | bytes 589824 | tf_op jit(solution)/shard_map/all_gather | solution.py:77
  42.5 9.5 fusion.6
  51.9 62.4 %reduce-scatter.23.cloned.1.call-done = f32[64,256]{1,0:T(8,128)} async-done(((f32[1024,256]{1,0:T(8,128)}), f32[64,256]{1,0:T(8,128)}) %reduce-scatter.23.cloned.1.call-update) | async-done | bytes 65552 | tf_op jit(solution)/shard_map/reduce_scatter | solution.py:26
  114.4 23.7 %all_gather.43 = f32[512,256]{1,0:T(8,128)S(1)} all-gather(f32[64,256]{1,0:T(8,128)} %reduce-scatter.23.cloned.1.call-done), channel_id=1, replica_groups=mesh['prow'=8,'pcol'=16] {'prow'}, dimensions={0}, use_global_device_ids=true | all-gather | bytes 589824 | tf_op jit(solution)/shard_map/all_gather | solution.py:109
  140.9 71.2 %reduce-scatter.25.cloned.1.call-done = f32[64,256]{1,0:T(8,128)} async-done(((f32[1024,256]{1,0:T(8,128)}), f32[64,256]{1,0:T(8,128)}) %reduce-scatter.25.cloned.1.call-update) | async-done | bytes 65552 | tf_op jit(solution)/shard_map/reduce_scatter | solution.py:26
  212.9 23.4 %all_gather.44 = f32[512,256]{1,0:T(8,128)S(1)} all-gather(f32[64,256]{1,0:T(8,128)S(1)} %bitcast_subtract_fusion.2), channel_id=1, replica_groups=mesh['prow'=8,'pcol'=16] {'prow'}, dimensions={0}, use_global_device_ids=true | all-gather | bytes 589824 | tf_op jit(solution)/shard_map/all_gather | solution.py:77
  245.2 66.9 %reduce-scatter.27.cloned.1.call-done = f32[64,256]{1,0:T(8,128)} async-done(((f32[1024,256]{1,0:T(8,128)}), f32[64,256]{1,0:T(8,128)}) %reduce-scatter.27.cloned.1.call-update) | async-done | bytes 65552 | tf_op jit(solution)/shard_map/reduce_scatter | solution.py:26
  312.1 23.5 %all_gather.45 = f32[512,256]{1,0:T(8,128)S(1)} all-gather(f32[64,256]{1,0:T(8,128)} %reduce-scatter.27.cloned.1.call-done), channel_id=1, replica_groups=mesh['prow'=8,'pcol'=16] {'prow'}, dimensions={0}, use_global_device_ids=true | all-gather | bytes 589824 | tf_op jit(solution)/shard_map/all_gather | solution.py:109
  340.4 71.5 %reduce-scatter.29.cloned.1.call-done = f32[64,256]{1,0:T(8,128)} async-done(((f32[1024,256]{1,0:T(8,128)}), f32[64,256]{1,0:T(8,128)}) %reduce-scatter.29.cloned.1.call-update) | async-done | bytes 65552 | tf_op jit(solution)/shard_map/reduce_scatter | solution.py:26
  412.8 23.1 %all_gather.46 = f32[512,256]{1,0:T(8,128)S(1)} all-gather(f32[64,256]{1,0:T(8,128)S(1)} %bitcast_subtract_fusion.1), channel_id=1, replica_groups=mesh['prow'=8,'pcol'=16] {'prow'}, dimensions={0}, use_global_device_ids=true | all-gather | bytes 589824 | tf_op jit(solution)/shard_map/all_gather | solution.py:77
  446.8 65.1 %reduce-scatter.31.cloned.1.call-done = f32[64,256]{1,0:T(8,128)} async-done(((f32[1024,256]{1,0:T(8,128)}), f32[64,256]{1,0:T(8,128)}) %reduce-scatter.31.cloned.1.call-update) | async-done | bytes 65552 | tf_op jit(solution)/shard_map/reduce_scatter | solution.py:26
  511.9 23.3 %all_gather.47 = f32[512,256]{1,0:T(8,128)S(1)} all-gather(f32[64,256]{1,0:T(8,128)} %reduce-scatter.31.cloned.1.call-done), channel_id=1, replica_groups=mesh['prow'=8,'pcol'=16] {'prow'}, dimensions={0}, use_global_device_ids=true | all-gather | bytes 589824 | tf_op jit(solution)/shard_map/all_gather | solution.py:109
  539.9 71.6 %reduce-scatter.33.cloned.1.call-done = f32[64,256]{1,0:T(8,128)} async-done(((f32[1024,256]{1,0:T(8,128)}), f32[64,256]{1,0:T(8,128)}) %reduce-scatter.33.cloned.1.call-update) | async-done | bytes 65552 | tf_op jit(solution)/shard_map/reduce_scatter | solution.py:26
  612.4 23.3 %all_gather.48 = f32[512,256]{1,0:T(8,128)S(1)} all-gather(f32[64,256]{1,0:T(8,128)S(1)} %bitcast_subtract_fusion), channel_id=1, replica_groups=mesh['prow'=8,'pcol'=16] {'prow'}, dimensions={0}, use_global_device_ids=true | all-gather | bytes 589824 | tf_op jit(solution)/shard_map/all_gather | solution.py:77
  640.1 71.6 %reduce-scatter.35.cloned.1.call-done = f32[64,256]{1,0:T(8,128)} async-done(((f32[1024,256]{1,0:T(8,128)}), f32[64,256]{1,0:T(8,128)}) %reduce-scatter.35.cloned.1.call-update) | async-done | bytes 65552 | tf_op jit(solution)/shard_map/reduce_scatter | solution.py:26
  711.8 48.8 %all-gather.9.cloned.1.call-done = f32[1024,256]{1,0:T(8,128)} async-done(((f32[64,256]{1,0:T(8,128)}), f32[1024,256]{1,0:T(8,128)}) %all-gather.9.cloned.1.call-update) | async-done | bytes 1048592 | tf_op jit(solution)/shard_map/all_gather | solution.py:86
  765.5 31.3 %reduce-scatter.43.cloned.1.call-done = f32[64,256]{1,0:T(8,128)} async-done(((f32[512,256]{1,0:T(8,128)}), f32[64,256]{1,0:T(8,128)}) %reduce-scatter.43.cloned.1.call-update) | async-done | bytes 65552 | tf_op jit(solution)/shard_map/reduce_scatter | solution.py:32
  796.9 51.2 %all-gather.11.cloned.1.call-done = f32[1024,256]{1,0:T(8,128)} async-done(((f32[64,256]{1,0:T(8,128)}), f32[1024,256]{1,0:T(8,128)}) %all-gather.11.cloned.1.call-update) | async-done | bytes 1048592 | tf_op jit(solution)/shard_map/all_gather | solution.py:123
  848.1 6.2 convolution_bitcast_fusion.7
  854.3 31.3 %reduce-scatter.37.cloned.1.call-done = f32[64,256]{1,0:T(8,128)} async-done(((f32[512,256]{1,0:T(8,128)}), f32[64,256]{1,0:T(8,128)}) %reduce-scatter.37.cloned.1.call-update) | async-done | bytes 65552 | tf_op jit(solution)/shard_map/reduce_scatter | solution.py:32
  887.1 50.6 %all-gather.13.cloned.1.call-done = f32[1024,256]{1,0:T(8,128)} async-done(((f32[64,256]{1,0:T(8,128)}), f32[1024,256]{1,0:T(8,128)}) %all-gather.13.cloned.1.call-update) | async-done | bytes 1048592 | tf_op jit(solution)/shard_map/all_gather | solution.py:86
  942.6 31.2 %reduce-scatter.45.cloned.1.call-done = f32[64,256]{1,0:T(8,128)} async-done(((f32[512,256]{1,0:T(8,128)}), f32[64,256]{1,0:T(8,128)}) %reduce-scatter.45.cloned.1.call-update) | async-done | bytes 65552 | tf_op jit(solution)/shard_map/reduce_scatter | solution.py:32
  974.3 50.8 %all-gather.15.cloned.1.call-done = f32[1024,256]{1,0:T(8,128)} async-done(((f32[64,256]{1,0:T(8,128)}), f32[1024,256]{1,0:T(8,128)}) %all-gather.15.cloned.1.call-update) | async-done | bytes 1048592 | tf_op jit(solution)/shard_map/all_gather | solution.py:123
  1025.1 5.5 fusion.10
  1035.1 31.3 %reduce-scatter.39.cloned.1.call-done = f32[64,256]{1,0:T(8,128)} async-done(((f32[512,256]{1,0:T(8,128)}), f32[64,256]{1,0:T(8,128)}) %reduce-scatter.39.cloned.1.call-update) | async-done | bytes 65552 | tf_op jit(solution)/shard_map/reduce_scatter | solution.py:32
  1067.9 50.6 %all-gather.17.cloned.1.call-done = f32[1024,256]{1,0:T(8,128)} async-done(((f32[64,256]{1,0:T(8,128)}), f32[1024,256]{1,0:T(8,128)}) %all-gather.17.cloned.1.call-update) | async-done | bytes 1048592 | tf_op jit(solution)/shard_map/all_gather | solution.py:86
  1125.3 31.2 %reduce-scatter.47.cloned.1.call-done = f32[64,256]{1,0:T(8,128)} async-done(((f32[512,256]{1,0:T(8,128)}), f32[64,256]{1,0:T(8,128)}) %reduce-scatter.47.cloned.1.call-update) | async-done | bytes 65552 | tf_op jit(solution)/shard_map/reduce_scatter | solution.py:32
  1156.8 51.0 %all-gather.19.cloned.1.call-done = f32[1024,256]{1,0:T(8,128)} async-done(((f32[64,256]{1,0:T(8,128)}), f32[1024,256]{1,0:T(8,128)}) %all-gather.19.cloned.1.call-update) | async-done | bytes 1048592 | tf_op jit(solution)/shard_map/all_gather | solution.py:123
  1220.5 31.3 %reduce-scatter.41.cloned.1.call-done = f32[64,256]{1,0:T(8,128)} async-done(((f32[512,256]{1,0:T(8,128)}), f32[64,256]{1,0:T(8,128)}) %reduce-scatter.41.cloned.1.call-update) | async-done | bytes 65552 | tf_op jit(solution)/shard_map/reduce_scatter | solution.py:32
  1253.6 50.3 %all-gather.21.cloned.1.call-done = f32[1024,256]{1,0:T(8,128)} async-done(((f32[64,256]{1,0:T(8,128)}), f32[1024,256]{1,0:T(8,128)}) %all-gather.21.cloned.1.call-update) | async-done | bytes 1048592 | tf_op jit(solution)/shard_map/all_gather | solution.py:86
  1309.9 30.3 %reduce-scatter.49.cloned.1.call-done = f32[64,256]{1,0:T(8,128)} async-done(((f32[512,256]{1,0:T(8,128)}), f32[64,256]{1,0:T(8,128)}) %reduce-scatter.49.cloned.1.call-update) | async-done | bytes 65552
  (109 shorter events, 89.0 us)
Async XLA Ops:
  7.2 7.0 slice-start
  7.2 107.2 %reduce-scatter.23.cloned.1.call-start = ((), (), s32[]{:S(2)}) async-start(), calls=%async_computation.14 | async-start | bytes 1114112 | tf_op jit(solution)/shard_map/reduce_scatter | solution.py:26
  14.2 28.2 %copy-start.4 = (f32[1,16,64,512]{3,2,1,0:T(8,128)}, f32[1,16,64,512]{3,2,1,0:T(8,128)S(1)}, u32[]{:S(2)}) copy-start(f32[1,16,64,512]{3,2,1,0:T(8,128)S(1)} %get-tuple-element.14) | copy-start | bytes 6291460
  42.4 169.7 %reduce-scatter.25.cloned.1.call-start = ((), (), s32[]{:S(2)}) async-start(), calls=%async_computation.15 | async-start | bytes 1114112 | tf_op jit(solution)/shard_map/reduce_scatter | solution.py:26
  138.0 74.0 %copy-start.10 = (f32[4,1,64,256]{3,2,1,0:T(8,128)S(1)}, f32[4,1,64,256]{3,2,1,0:T(8,128)}, u32[]{:S(2)}) copy-start(f32[4,1,64,256]{3,2,1,0:T(8,128)} %param.3) | copy-start | bytes 786436
  140.9 171.3 %reduce-scatter.27.cloned.1.call-start = ((), (), s32[]{:S(2)}) async-start(), calls=%async_computation.16 | async-start | bytes 1114112 | tf_op jit(solution)/shard_map/reduce_scatter | solution.py:26
  240.8 171.2 %reduce-scatter.29.cloned.1.call-start = ((), (), s32[]{:S(2)}) async-start(), calls=%async_computation.17 | async-start | bytes 1114112 | tf_op jit(solution)/shard_map/reduce_scatter | solution.py:26
  340.3 171.5 %reduce-scatter.31.cloned.1.call-start = ((), (), s32[]{:S(2)}) async-start(), calls=%async_computation.18 | async-start | bytes 1114112 | tf_op jit(solution)/shard_map/reduce_scatter | solution.py:26
  440.3 171.3 %reduce-scatter.33.cloned.1.call-start = ((), (), s32[]{:S(2)}) async-start(), calls=%async_computation.19 | async-start | bytes 1114112 | tf_op jit(solution)/shard_map/reduce_scatter | solution.py:26
  539.9 171.9 %reduce-scatter.35.cloned.1.call-start = ((), (), s32[]{:S(2)}) async-start(), calls=%async_computation.20 | async-start | bytes 1114112 | tf_op jit(solution)/shard_map/reduce_scatter | solution.py:26
  640.0 120.6 %all-gather.9.cloned.1.call-start = ((), (), s32[]{:S(2)}) async-start(), calls=%async_computation.21 | async-start | bytes 1114112 | tf_op jit(solution)/shard_map/all_gather | solution.py:86
  711.8 85.1 %reduce-scatter.43.cloned.1.call-start = ((), (), s32[]{:S(2)}) async-start(), calls=%async_computation.31 | async-start | bytes 589824 | tf_op jit(solution)/shard_map/reduce_scatter | solution.py:32
  765.5 82.6 %all-gather.11.cloned.1.call-start = ((), (), s32[]{:S(2)}) async-start(), calls=%async_computation.22 | async-start | bytes 1114112 | tf_op jit(solution)/shard_map/all_gather | solution.py:123
  796.8 88.7 %copy-start.9 = (f32[64,256]{1,0:T(8,128)S(1)}, f32[64,256]{1,0:T(8,128)}, u32[]{:S(2)}) copy-start(f32[64,256]{1,0:T(8,128)} %reduce-scatter.31.cloned.1.call-done) | copy-start | bytes 196612
  796.9 88.7 %reduce-scatter.37.cloned.1.call-start = ((), (), s32[]{:S(2)}) async-start(), calls=%async_computation.23 | async-start | bytes 589824 | tf_op jit(solution)/shard_map/reduce_scatter | solution.py:32
  854.3 83.4 %all-gather.13.cloned.1.call-start = ((), (), s32[]{:S(2)}) async-start(), calls=%async_computation.24 | async-start | bytes 1114112 | tf_op jit(solution)/shard_map/all_gather | solution.py:86
  887.1 86.8 %reduce-scatter.45.cloned.1.call-start = ((), (), s32[]{:S(2)}) async-start(), calls=%async_computation.32 | async-start | bytes 589824 | tf_op jit(solution)/shard_map/reduce_scatter | solution.py:32
  942.5 88.1 %copy-start.5 = (f32[1024,256]{1,0:T(8,128)S(1)}, f32[1024,256]{1,0:T(8,128)}, u32[]{:S(2)}) copy-start(f32[1024,256]{1,0:T(8,128)} %all-gather.11.cloned.1.call-done) | copy-start | bytes 3145732
  942.6 82.6 %all-gather.15.cloned.1.call-start = ((), (), s32[]{:S(2)}) async-start(), calls=%async_computation.25 | async-start | bytes 1114112 | tf_op jit(solution)/shard_map/all_gather | solution.py:123
  973.9 92.5 %reduce-scatter.39.cloned.1.call-start = ((), (), s32[]{:S(2)}) async-start(), calls=%async_computation.26 | async-start | bytes 589824 | tf_op jit(solution)/shard_map/reduce_scatter | solution.py:32
  1025.1 5.5 copy-start.3
  1030.7 35.7 %copy-start.8 = (f32[64,256]{1,0:T(8,128)S(1)}, f32[64,256]{1,0:T(8,128)}, u32[]{:S(2)}) copy-start(f32[64,256]{1,0:T(8,128)} %reduce-scatter.27.cloned.1.call-done) | copy-start | bytes 196612
  1035.1 83.4 %all-gather.17.cloned.1.call-start = ((), (), s32[]{:S(2)}) async-start(), calls=%async_computation.27 | async-start | bytes 1114112 | tf_op jit(solution)/shard_map/all_gather | solution.py:86
  1067.9 88.7 %reduce-scatter.47.cloned.1.call-start = ((), (), s32[]{:S(2)}) async-start(), calls=%async_computation.33 | async-start | bytes 589824 | tf_op jit(solution)/shard_map/reduce_scatter | solution.py:32
  1125.2 82.6 %all-gather.19.cloned.1.call-start = ((), (), s32[]{:S(2)}) async-start(), calls=%async_computation.28 | async-start | bytes 1114112 | tf_op jit(solution)/shard_map/all_gather | solution.py:123
  1156.6 95.2 %reduce-scatter.41.cloned.1.call-start = ((), (), s32[]{:S(2)}) async-start(), calls=%async_computation.29 | async-start | bytes 589824 | tf_op jit(solution)/shard_map/reduce_scatter | solution.py:32
  1216.2 35.6 %copy-start.7 = (f32[64,256]{1,0:T(8,128)S(1)}, f32[64,256]{1,0:T(8,128)}, u32[]{:S(2)}) copy-start(f32[64,256]{1,0:T(8,128)} %reduce-scatter.23.cloned.1.call-done) | copy-start | bytes 196612
  1220.5 83.4 %all-gather.21.cloned.1.call-start = ((), (), s32[]{:S(2)}) async-start(), calls=%async_computation.30 | async-start | bytes 1114112 | tf_op jit(solution)/shard_map/all_gather | solution.py:86
  1253.3 55.5 %copy-start.14 = (f32[64,256]{1,0:T(8,128)S(1)}, f32[64,256]{1,0:T(8,128)}, u32[]{:S(2)}) copy-start(f32[64,256]{1,0:T(8,128)} %reduce-scatter.35.cloned.1.call-done) | copy-start | bytes 196612
  1253.3 56.2 %copy-start.11 = (f32[64,256]{1,0:T(8,128)S(1)}, f32[64,256]{1,0:T(8,128)}, u32[]{:S(2)}) copy-start(f32[64,256]{1,0:T(8,128)} %reduce-scatter.43.cloned.1.call-done) | copy-start | bytes 196612
  1253.3 56.3 %copy-start.12 = (f32[64,256]{1,0:T(8,128)S(1)}, f32[64,256]{1,0:T(8,128)}, u32[]{:S(2)}) copy-start(f32[64,256]{1,0:T(8,128)} %reduce-scatter.45.cloned.1.call-done) | copy-start | bytes 196612
  1253.3 86.8 %reduce-scatter.49.cloned.1.call-start = ((), (), s32[]{:S(2)}) async-start(), calls=%async_computation.34 | async-start | bytes 589824
  (5 other events, 18.8 us)
Sparse Core Ops, SparseCore 0:
  42.5 71.7 reduce-scatter.22
  141.0 71.0 reduce-scatter.24
  240.9 71.2 reduce-scatter.26
  340.5 71.4 reduce-scatter.28
  440.4 71.4 reduce-scatter.30
  540.0 71.4 reduce-scatter.32
  640.2 71.5 reduce-scatter.34
  714.5 46.0 all-gather.8
  765.6 31.1 reduce-scatter.42
  799.1 48.8 all-gather.10
  854.4 31.1 reduce-scatter.36
  888.8 48.8 all-gather.12
  942.7 31.1 reduce-scatter.44
  976.2 48.8 all-gather.14
  1035.2 31.1 reduce-scatter.38
  1069.6 48.8 all-gather.16
  1125.4 31.1 reduce-scatter.46
  1158.9 48.8 all-gather.18
  1220.6 31.1 reduce-scatter.40
  1255.0 48.8 all-gather.20
  1308.9 31.1 reduce-scatter.48
where the time goes:
time: 1360 us; the launch traced here: 1350 us
  waiting for transfers between devices  1050 us (77%)
  blocking collectives  166 us (12%)
  matrix products  83.7 us (6%)
  local copies, waits for them, and re-layouts  23.6 us (2%)
  between operations  14.8 us (1%)
    reduce_scatter x7, waiting for transfers between devices, sum_columns(): lax.psum_scatter(term(jnp.int32(0), piece * lax.axis_size('pcol')), 'pcol...  480 us
    all_gather x4, waiting for transfers between devices, apply_inverse_transposed(): lax.all_gather(reduced, 'pcol', axis=0, tiled=True)  200 us
    reduce_scatter x6, waiting for transfers between devices, sum_rows(): lax.psum_scatter(term(jnp.int32(0), piece * lax.axis_size('prow')), 'prow...  188 us
    all_gather x3, waiting for transfers between devices, local(): lax.all_gather(solved, 'pcol', axis=0, tiled=True)  153 us
    all_gather x4, blocking collectives, apply_inverse(): lax.all_gather(reduced, 'prow', axis=0, tiled=True)  95.2 us
    all_gather x3, blocking collectives, local(): lax.all_gather(solved, 'prow', axis=0, tiled=True)  70.5 us
    dot_general x10, matrix products, product_left(): lax.dot_general(left, right, (((0,), (0,)), ((), ())), precision=lax.Prec...  44.8 us
    dot_general x10, matrix products, product(): jnp.dot(left, right, precision=lax.Precision.HIGHEST, preferred_element_t...  38.9 us
  transfers between devices with their start and end apart: 21, of which 21 were waited for; matrix products, arithmetic and copies ran while one was open for 2% of the time, Pallas kernels for 0%

commit v1 on v0

v1 whole, which is shorter than its diff:
```python
import jax
import jax.numpy as jnp
from jax import lax
from jax.experimental import pallas as pl
from jax.experimental.pallas import tpu as pltpu
from jax.sharding import PartitionSpec as P

MESH = pl.DeviceIdType.MESH
F32 = jnp.float32
BF16 = jnp.bfloat16

SLOTS = 4
TILES = [
    ("E", 0), ("L", 1, 0), ("L", 2, 0), ("L", 3, 0), ("E", 1),
    ("L", 2, 1), ("L", 3, 1), ("E", 2), ("L", 3, 2), ("E", 3),
]
TILE = {name: index for index, name in enumerate(TILES)}


def dot(a, b):
    return lax.dot_general(a, b, (((1,), (0,)), ((), ())), preferred_element_type=F32)


def dot_t(a, b):
    return lax.dot_general(a, b, (((0,), (0,)), ((), ())), preferred_element_type=F32)


def split(value):
    high = value.astype(BF16)
    return high, (value - high.astype(F32)).astype(BF16)


def kernel(
    k_ref, l_ref, e_ref, y_ref, x_ref,
    stage, mh, ml, u, v, cbuf, rbuf, g, bh, bl, facc,
    gb, ch_, cl_, w, wbuf, bacc,
    ld_sem, core_s, core_r, rs_s, rs_r, ag_s, ag_r,
    bag_s, bag_r, rel_s, rel_r, brs_s, brs_r,
):
    r = lax.axis_index("prow")
    p = lax.axis_index("pcol")
    c = lax.rem(p, 2)
    q = p // 2
    mate = (r, p + 1 - 2 * c)

    def peer(other):
        return (r, 2 * other + c)

    def turn(base, step, n):
        return lax.rem(base + step, n)

    def load(i, rel):
        name = TILES[i]
        s = i % SLOTS
        half = 1 - c if rel == 0 else c
        if name[0] == "E":
            src = e_ref.at[name[1], :, half]
        else:
            src = l_ref.at[name[1] * (name[1] - 1) // 2 + name[2], :, half]
        return pltpu.make_async_copy(src, stage.at[s, rel], ld_sem.at[s, rel])

    def convert(i):
        s = i % SLOTS
        for rel in range(2):
            load(i, rel).wait()

            @pl.loop(0, 8)
            def _(a):
                high, low = split(stage[s, rel, a])
                rows = pl.ds(pl.multiple_of(a * 64, 64), 64)
                mh[i, rel, rows, :] = high
                ml[i, rel, rows, :] = low

        if i + SLOTS < len(TILES):
            for rel in range(2):
                load(i + SLOTS, rel).start()

    for i in range(SLOTS):
        for rel in range(2):
            load(i, rel).start()

    barrier = pltpu.get_barrier_semaphore()
    pl.semaphore_signal(barrier, inc=1, device_id=mate, device_id_type=MESH)
    for j in range(1, 8):
        pl.semaphore_signal(barrier, inc=1, device_id=peer(turn(q, j, 8)), device_id_type=MESH)
        pl.semaphore_signal(barrier, inc=1, device_id=(turn(r, j, 8), p), device_id_type=MESH)
    pl.semaphore_wait(barrier, 15)

    def remote(src, dst, send, recv, device):
        return pltpu.make_async_remote_copy(
            src_ref=src, dst_ref=dst, send_sem=send, recv_sem=recv, device_id=device, device_id_type=MESH
        )

    def gemm(i, rel, rows, b):
        ah, al = mh[i, rel, rows, :], ml[i, rel, rows, :]
        return dot(ah, bh[b]) + dot(ah, bl[b]) + dot(al, bh[b])

    def pair_rows(pair):
        return pl.ds(pl.multiple_of(pair * 128, 128), 128)

    def fwd_filler(i, b, slot, first):
        def run():
            for rel in range(2):

                @pl.loop(0, 4)
                def _(pair):
                    rows = pair_rows(pair)
                    out = gemm(i, rel, rows, b)
                    facc[slot, rel, rows, :] = out if first else facc[slot, rel, rows, :] + out

        return run

    def fwd_rs(t, i, b, slot, fillers):
        par = t % 2
        home = q // 2

        def core(pair, j):
            rows = pair_rows(pair)
            return remote(u.at[par, rows], cbuf.at[par, rows], core_s.at[par, j], core_r.at[par, j], mate)

        pairs = [turn(home, j, 4) for j in (1, 2, 3, 0)]
        for j, pair in enumerate(pairs):
            rows = pair_rows(pair)
            out = gemm(i, 0, rows, b)
            u[par, rows, :] = out if slot is None else out + facc[slot, 0, rows, :]
            core(pair, j).start()
        for j, pair in enumerate(pairs):
            rows = pair_rows(pair)
            out = gemm(i, 1, rows, b)
            v[par, rows, :] = out if slot is None else out + facc[slot, 1, rows, :]

        def message(other):
            rows = pl.ds(pl.multiple_of(other * 64, 64), 64)
            return remote(
                v.at[par, rows], rbuf.at[par, q], rs_s.at[par, other], rs_r.at[par, q], peer(other)
            )

        for j, pair in enumerate(pairs):
            rows = pair_rows(pair)
            core(pair, j).wait_recv()
            v[par, rows, :] = v[par, rows, :] + cbuf[par, rows, :]
            if j < 3:
                message(2 * pair).start()
                message(2 * pair + 1).start()
            else:
                message(q + 1 - 2 * lax.rem(q, 2)).start()
        for run in fillers:
            run()
        total = v[par, pl.ds(pl.multiple_of(q * 64, 64), 64), :]
        for j in range(1, 8):
            s = turn(q, j, 8)
            remote(rbuf.at[par, s], rbuf.at[par, s], rs_s.at[par, s], rs_r.at[par, s], mate).wait_recv()
            total = total + rbuf[par, s]
        for j, pair in enumerate(pairs):
            core(pair, j).wait_send()
        for j in range(1, 8):
            message(turn(q, j, 8)).wait_send()
        return total

    def fwd_ag(t, value, b, fillers):
        par = t % 2
        g[t, r] = value

        def message(j):
            return remote(
                g.at[t, r], g.at[t, r], ag_s.at[par, j], ag_r.at[par, r], (turn(r, j, 8), p)
            )

        for j in range(1, 8):
            message(j).start()
        for run in fillers:
            run()
        for j in range(8):
            s = turn(r, j, 8)
            if j > 0:
                remote(g.at[t, s], g.at[t, s], ag_s.at[par, j], ag_r.at[par, s], mate).wait_recv()
            rows = pl.ds(pl.multiple_of(s * 64, 64), 64)
            high, low = split(g[t, s])
            bh[b, rows, :] = high
            bl[b, rows, :] = low
        for j in range(1, 8):
            message(j).wait_send()

    def conv(*names):
        return [lambda i=TILE[name]: convert(i) for name in names]

    fwd_ag(0, k_ref[0], 0, conv(("E", 0), ("L", 1, 0)))
    late = {0: conv(("L", 2, 0), ("L", 3, 0)), 1: conv(("L", 3, 1),), 2: conv(("E", 3)), 3: []}
    fill_rs = {
        0: [fwd_filler(TILE["L", 2, 0], 1, 0, True)],
        1: [fwd_filler(TILE["L", 3, 1], 1, 1, False)],
        2: [],
    }
    fill_ag = {
        0: [fwd_filler(TILE["L", 3, 0], 1, 1, True)] + conv(("E", 1), ("L", 2, 1)),
        1: conv(("E", 2), ("L", 3, 2)),
        2: [],
    }
    for k in range(4):
        y_ref[k] = fwd_rs(2 * k, TILE["E", k], 0, None, late[k])
        if k < 3:
            fwd_ag(2 * k + 1, y_ref[k], 1, [])
            slot = None if k == 0 else k - 1
            down = fwd_rs(2 * k + 1, TILE["L", k + 1, k], 1, slot, fill_rs[k])
            fwd_ag(2 * k + 2, k_ref[k + 1] - down, 0, fill_ag[k])

    def gemm_t(i, rel, cols, b):
        ah, al = mh[i, rel, :, cols], ml[i, rel, :, cols]
        return dot_t(ah, ch_[b, rel]) + dot_t(ah, cl_[b, rel]) + dot_t(al, ch_[b, rel])

    def bwd_ag(t, value, b, fillers):
        par = t % 2
        gb[t, 1, q] = value

        def message(j):
            return remote(
                gb.at[t, 1, q], gb.at[t, 1, q], bag_s.at[par, j], bag_r.at[par, q], peer(turn(q, j, 8))
            )

        def relay(s):
            return remote(gb.at[t, 1, s], gb.at[t, 0, s], rel_s.at[par, s], rel_r.at[par, s], mate)

        def take(rel, s):
            rows = pl.ds(pl.multiple_of(s * 64, 64), 64)
            high, low = split(gb[t, rel, s])
            ch_[b, rel, rows, :] = high
            cl_[b, rel, rows, :] = low

        for j in range(1, 8):
            message(j).start()
        relay(q).start()
        for run in fillers:
            run()
        for j in range(8):
            s = turn(q, j, 8)
            if j > 0:
                remote(gb.at[t, 1, s], gb.at[t, 1, s], bag_s.at[par, j], bag_r.at[par, s], mate).wait_recv()
                relay(s).start()
            take(1, s)
        for j in range(8):
            s = turn(q, j, 8)
            relay(s).wait_recv()
            take(0, s)
        for j in range(1, 8):
            message(j).wait_send()
        for j in range(8):
            relay(turn(q, j, 8)).wait_send()

    def bwd_filler(i, b, slot, first):
        def run():
            for pair in range(4):
                cols = pl.ds(pair * 128, 128)
                out = gemm_t(i, 0, cols, b) + gemm_t(i, 1, cols, b)
                bacc[slot, cols, :] = out if first else bacc[slot, cols, :] + out

        return run

    def bwd_rs(t, i, b, slot, fillers):
        par = t % 2

        def message(j):
            other = turn(r, j, 8)
            rows = pl.ds(pl.multiple_of(other * 64, 64), 64)
            return remote(
                w.at[par, rows], wbuf.at[par, r], brs_s.at[par, j], brs_r.at[par, r], (other, p)
            )

        for pair in range(4):
            cols = pl.ds(pair * 128, 128)
            out = gemm_t(i, 0, cols, b) + gemm_t(i, 1, cols, b)
            w[par, cols, :] = out if slot is None else out + bacc[slot, cols, :]
        for j in range(1, 8):
            message(j).start()
        for run in fillers:
            run()
        total = w[par, pl.ds(pl.multiple_of(r * 64, 64), 64), :]
        for j in range(1, 8):
            s = turn(r, j, 8)
            remote(wbuf.at[par, s], wbuf.at[par, s], brs_s.at[par, j], brs_r.at[par, s], mate).wait_recv()
            total = total + wbuf[par, s]
        for j in range(1, 8):
            message(j).wait_send()
        return total

    back_rs = {
        3: [bwd_filler(TILE["L", 3, 1], 1, 1, True)],
        2: [bwd_filler(TILE["L", 2, 0], 1, 0, False)],
        1: [],
    }
    back_ag = {3: [bwd_filler(TILE["L", 3, 0], 1, 0, True)], 2: [], 1: []}
    t = 0
    bwd_ag(0, y_ref[3], 0, [])
    for k in range(3, -1, -1):
        x_ref[k] = bwd_rs(t, TILE["E", k], 0, None, [])
        if k > 0:
            bwd_ag(t + 1, x_ref[k], 1, [])
            slot = None if k == 3 else k - 1
            up = bwd_rs(t + 1, TILE["L", k, k - 1], 1, slot, back_rs[k])
            bwd_ag(t + 2, y_ref[k - 1] - up, 0, back_ag[k])
            t += 2


def local(k_star, lower_blocks, diag_inverse):
    steps, _, piece, cols = k_star.shape
    pairs, groups, _, width = lower_blocks.shape
    dma = pltpu.SemaphoreType.DMA
    n = len(TILES)
    y, x = pl.pallas_call(
        kernel,
        out_shape=[jax.ShapeDtypeStruct((steps, piece, cols), F32)] * 2,
        in_specs=[
            pl.BlockSpec(memory_space=pltpu.VMEM),
            pl.BlockSpec(memory_space=pl.ANY),
            pl.BlockSpec(memory_space=pl.ANY),
        ],
        out_specs=[pl.BlockSpec(memory_space=pltpu.VMEM)] * 2,
        scratch_shapes=[
            pltpu.VMEM((SLOTS, 2, 8, 64, 512), F32),
            pltpu.VMEM((n, 2, 512, 512), BF16),
            pltpu.VMEM((n, 2, 512, 512), BF16),
            pltpu.VMEM((2, 512, 256), F32),
            pltpu.VMEM((2, 512, 256), F32),
            pltpu.VMEM((2, 512, 256), F32),
            pltpu.VMEM((2, 8, 64, 256), F32),
            pltpu.VMEM((7, 8, 64, 256), F32),
            pltpu.VMEM((2, 512, 256), BF16),
            pltpu.VMEM((2, 512, 256), BF16),
            pltpu.VMEM((2, 2, 512, 256), F32),
            pltpu.VMEM((7, 2, 8, 64, 256), F32),
            pltpu.VMEM((2, 2, 512, 256), BF16),
            pltpu.VMEM((2, 2, 512, 256), BF16),
            pltpu.VMEM((2, 512, 256), F32),
            pltpu.VMEM((2, 8, 64, 256), F32),
            pltpu.VMEM((2, 512, 256), F32),
            dma((SLOTS, 2)),
            dma((2, 4)), dma((2, 4)),
            dma((2, 8)), dma((2, 8)),
            dma((2, 8)), dma((2, 8)),
            dma((2, 8)), dma((2, 8)),
            dma((2, 8)), dma((2, 8)),
            dma((2, 8)), dma((2, 8)),
        ],
        compiler_params=pltpu.CompilerParams(
            collective_id=0, has_side_effects=True, vmem_limit_bytes=60 * 1024 * 1024
        ),
    )(
        k_star.reshape(steps, piece, cols),
        lower_blocks.reshape(pairs, groups // 2, 2, piece, width),
        diag_inverse.reshape(steps, groups // 2, 2, piece, width),
    )
    shape = (steps, 1, piece, cols)
    return y.reshape(shape), x.reshape(shape)


def solution(mesh):
    return jax.shard_map(
        local,
        mesh=mesh,
        in_specs=(
            P(None, "pcol", "prow", None),
            P(None, None, "prow", "pcol"),
            P(None, None, "prow", "pcol"),
        ),
        out_specs=(P(None, "pcol", "prow", None), P(None, "pcol", "prow", None)),
        check_vma=False,
    )
```

time: 1360 us -> 289 us (0.21)
  waiting for transfers between devices: 1050 us -> 0 us
  Pallas kernels: 0 us -> 285 us
  blocking collectives: 166 us -> 0 us
  matrix products: 83.7 us -> 0 us
  local copies, waits for them, and re-layouts: 23.6 us -> 3.35 us
  between operations: 14.8 us -> 0.64 us
    reduce_scatter x13 -> x0, waiting for transfers between devices: 668 us -> none  [the longest x7 480 us: sum_columns(): lax.psum_scatter(term(jnp.int32(0), piece * lax.axis_size('pcol')), 'pcol...]
    all_gather x7 -> x0, waiting for transfers between devices: 353 us -> none  [the longest x4 200 us: apply_inverse_transposed(): lax.all_gather(reduced, 'pcol', axis=0, tiled=True)]
    pallas_call x0 -> x1, Pallas kernels: none -> 285 us  [local(): pl.pallas_call(kernel, out_shape=[jax.ShapeDtypeStruct((steps, piece, col...]
    all_gather x7 -> x0, blocking collectives: 166 us -> none  [the longest x4 95.2 us: apply_inverse(): lax.all_gather(reduced, 'prow', axis=0, tiled=True)]
    dot_general x20 -> x0, matrix products: 83.7 us -> none  [the longest x10 44.8 us: product_left(): lax.dot_general(left, right, (((0,), (0,)), ((), ())), precision=lax.Prec...]
    unnamed x22 -> x0, waiting for transfers between devices: 30.7 us -> none
    slice x4 -> x0, local copies, waits for them, and re-layouts: 16.4 us -> none  [the longest x1 9.47 us: term(): rows = lower[pair_index(block, other)]]
  transfers between devices with their start and end apart: 21 -> 0, of which waited for: 21 -> 0; matrix products, arithmetic and copies ran while one was open for 2% -> 0% of each run, Pallas kernels for 0% -> 0%
where the time goes in v1:
time: 289 us
  Pallas kernels  285 us (99%)
  local copies, waits for them, and re-layouts  3.35 us (1%)
    pallas_call x1, Pallas kernels, local(): pl.pallas_call(kernel, out_shape=[jax.ShapeDtypeStruct((steps, piece, col...  285 us

profile of v1, /device:TPU:1, one launch (start us, length us, event | category | flops | bytes accessed | tf_op | source)
XLA Modules:
  0.0 289.3 jit_solution(2300970130742808422)
XLA Ops:
  0.6 285.3 %shard_map.50 = (f32[4,64,256]{2,1,0:T(8,128)}, f32[4,64,256]{2,1,0:T(8,128)}) custom-call(f32[4,64,256]{2,1,0:T(8,128)} %bitcast.13, f32[6,8,2,64,512]{4,3,2,1,0:T(8,128)} %bitcast.9, f32[4,8,2,64,512]{4,3,2,1,0:T(8,128)} %bitcast.10), custom_call_target="tpu_custom_call" | custom-call | tf_op jit(solution)/shard_map/pallas_call | solution.py:308
  285.9 1.7 copy.9
  287.6 1.7 copy.10

commit v2 on v0

v2 whole, which is shorter than its diff:
```python
import jax
import jax.numpy as jnp
from jax import lax
from jax.experimental import pallas as pl
from jax.experimental.pallas import tpu as pltpu
from jax.sharding import PartitionSpec as P

MESH = pl.DeviceIdType.MESH
F32 = jnp.float32
BF16 = jnp.bfloat16

SLOTS = 4
CHUNK = 256
TILES = [
    ("E", 0), ("L", 1, 0), ("E", 1), ("L", 2, 1), ("L", 2, 0),
    ("L", 3, 0), ("E", 2), ("L", 3, 2), ("L", 3, 1), ("E", 3),
]
TILE = {name: index for index, name in enumerate(TILES)}
HALVES = 2 * len(TILES)
FAR_FIRST = [(1, 2), (1, 1), (1, 3), (0, 2), (1, 0), (0, 1), (0, 3)]


def dot(a, b):
    return lax.dot_general(a, b, (((1,), (0,)), ((), ())), preferred_element_type=F32)


def dot_t(a, b):
    return lax.dot_general(a, b, (((0,), (0,)), ((), ())), preferred_element_type=F32)


def split(value):
    high = value.astype(BF16)
    return high, (value - high.astype(F32)).astype(BF16)


def kernel(
    k_ref, l_ref, e_ref, y_ref, x_ref,
    stage, mh, ml, part, acc, ops, gf, gb, rf, rb, ksend, krecv, kx, yfull, xfull, ybuf, xbuf,
    ld_sem, mate_s, mate_r, free, io_s, io_r,
    rs_s, rs_r, ag_s, ag_r, brs_s, brs_r, bag_s, bag_r,
):
    r = lax.axis_index("prow")
    p = lax.axis_index("pcol")
    c = lax.rem(p, 2)
    q = p // 2
    mate = (r, p + 1 - 2 * c)

    def member(me, offset):
        return lax.rem(me // 4 + offset[0], 2) * 4 + lax.rem(lax.rem(me, 4) + offset[1], 4)

    def on_q(offset):
        return (r, 2 * member(q, offset) + c)

    def on_r(offset):
        return (member(r, offset), p)

    def remote(src, dst, send, recv, device):
        return pltpu.make_async_remote_copy(
            src_ref=src, dst_ref=dst, send_sem=send, recv_sem=recv, device_id=device, device_id_type=MESH
        )

    def source(n):
        name, half = TILES[n // 2], n % 2
        if name[0] == "E":
            return e_ref.at[name[1], :, half]
        return l_ref.at[name[1] * (name[1] - 1) // 2 + name[2], :, half]

    def own(n):
        s = n % SLOTS
        return pltpu.make_async_copy(source(n), stage.at[s, c], ld_sem.at[s])

    def shared(n):
        s = n % SLOTS
        return remote(source(n), stage.at[s, c], mate_s.at[s], mate_r.at[s], mate)

    def convert(n):
        s = n % SLOTS
        own(n).wait()
        shared(n).wait()
        for kh in range(2):

            @pl.loop(0, 8)
            def _(a):
                high, low = split(stage[s, kh, a])
                rows = pl.ds(pl.multiple_of(a * 64, 64), 64)
                mh[n // 2, kh, n % 2, rows, :] = high
                ml[n // 2, kh, n % 2, rows, :] = low

        if n + SLOTS < HALVES:
            pl.semaphore_signal(free, inc=1, device_id=mate, device_id_type=MESH)
        following = n - 1 + SLOTS
        if n >= 1 and following < HALVES:
            pl.semaphore_wait(free, 1)
            own(following).start()
            shared(following).start()

    for n in range(SLOTS):
        own(n).start()
    for k in range(4):
        left, right = k_ref[k, :, 0:128], k_ref[k, :, 128:256]
        kx[k, c] = jnp.where(c == 0, left, right)
        ksend[k] = jnp.where(c == 0, right, left)

    barrier = pltpu.get_barrier_semaphore()
    pl.semaphore_signal(barrier, inc=1, device_id=mate, device_id_type=MESH)
    for offset in FAR_FIRST:
        pl.semaphore_signal(barrier, inc=1, device_id=on_q(offset), device_id_type=MESH)
        pl.semaphore_signal(barrier, inc=1, device_id=on_r(offset), device_id_type=MESH)
    pl.semaphore_wait(barrier, 15)

    columns = remote(ksend, krecv, io_s.at[8], io_r.at[8], mate)
    columns.start()
    for n in range(SLOTS):
        shared(n).start()
    columns.wait()
    for k in range(4):
        kx[k, 1 - c] = krecv[k]

    class Forward:
        g, rbuf, me, sum_me = gf, rf, r, q
        ag, rs = (ag_s, ag_r), (rs_s, rs_r)
        on_ag, on_rs = staticmethod(on_r), staticmethod(on_q)

        @staticmethod
        def product(i, kh, oh, b, at):
            rows = pl.ds(at, CHUNK)
            wide = dot(mh[i, kh, oh, rows, :], ops[b, kh])
            return wide[:, 0:128] + wide[:, 128:256] + dot(ml[i, kh, oh, rows, :], ops[b, kh, :, 0:128])

    class Backward:
        g, rbuf, me, sum_me = gb, rb, q, r
        ag, rs = (bag_s, bag_r), (brs_s, brs_r)
        on_ag, on_rs = staticmethod(on_q), staticmethod(on_r)

        @staticmethod
        def product(i, kh, oh, b, at):
            cols = pl.ds(at, CHUNK)
            wide = dot_t(mh[i, oh, kh, :, cols], ops[b, kh])
            return wide[:, 0:128] + wide[:, 128:256] + dot_t(ml[i, oh, kh, :, cols], ops[b, kh, :, 0:128])

    PER = CHUNK // 64

    def chunks():
        return range(0, 512, CHUNK)

    def groups(value):
        return value.reshape(PER, 64, 128)

    def gather_start(way, par, h, value):
        way.g[par, h, way.me] = value
        for offset in FAR_FIRST:
            remote(
                way.g.at[par, h, way.me], way.g.at[par, h, way.me],
                way.ag[0].at[par, h], way.ag[1].at[par, h], way.on_ag(offset),
            ).start()

    def seven(buf, sems, par, h):
        view = buf.at[par, h, pl.ds(0, 7)]
        return remote(view, view, sems[0].at[par, h], sems[1].at[par, h], mate)

    def gather_finish(way, par, h, b):
        seven(way.g, way.ag, par, h).wait_recv()
        high, low = split(way.g[par, h].reshape(512, 128))
        ops[b, h, :, 0:128] = high
        ops[b, h, :, 128:256] = low

    def sum_start(way, par, h):
        for j, offset in enumerate(FAR_FIRST):
            remote(
                part.at[par, h, member(way.sum_me, offset)], way.rbuf.at[par, h, j],
                way.rs[0].at[par, h], way.rs[1].at[par, h], way.on_rs(offset),
            ).start()

    def sum_finish(way, par, h):
        total = part[par, h, way.sum_me]
        seven(way.rbuf, way.rs, par, h).wait_recv()
        for j in range(7):
            total = total + way.rbuf[par, h, j]
        return total

    def aside(way, i, b, slot, first):
        def run(oh):
            for at in chunks():
                out = way.product(i, 0, oh, b, at) + way.product(i, 1, oh, b, at)
                where = pl.ds(at // 64, PER)
                out = groups(out)
                acc[slot, oh, where] = out if first else acc[slot, oh, where] + out

        return [lambda oh=oh: run(oh) for oh in range(2)]

    def step(way, t, i, b, slot, after, summing, gathering):
        par = t % 2
        gather_finish(way, par, 0, b)
        for oh in range(2):
            for at in chunks():
                where = pl.ds(at // 64, PER)
                out = groups(way.product(i, 0, oh, b, at))
                part[par, oh, where] = out if slot is None else out + acc[slot, oh, where]
        gather_finish(way, par, 1, b)
        for oh in range(2):
            for at in chunks():
                where = pl.ds(at // 64, PER)
                part[par, oh, where] = part[par, oh, where] + groups(way.product(i, 1, oh, b, at))
            sum_start(way, par, oh)
        for h in range(2):
            seven(way.g, way.ag, par, h).wait_send()
        for run in summing:
            run()
        for h in range(2):
            after(h, sum_finish(way, par, h))
        for run in gathering:
            run()
        for h in range(2):
            seven(way.rbuf, way.rs, par, h).wait_send()

    def hand_over(full, buf, k, sem):
        return remote(full.at[k, 1 - c], buf.at[k], io_s.at[sem], io_r.at[sem], mate)

    def conv(*names):
        return [lambda n=n: convert(n) for name in names for n in (2 * TILE[name], 2 * TILE[name] + 1)]

    for h in range(2):
        gather_start(Forward, 0, h, kx[0, h])
    for run in conv(("E", 0)):
        run()
    fill = {
        ("E", 0): (conv(("L", 1, 0)), conv(("E", 1))),
        ("L", 0): (conv(("L", 2, 1)), conv(("L", 2, 0))),
        ("E", 1): (aside(Forward, TILE["L", 2, 0], 1, 0, True), conv(("L", 3, 0))),
        ("L", 1): (conv(("E", 2)), aside(Forward, TILE["L", 3, 0], 1, 1, True) + conv(("L", 3, 2))),
        ("E", 2): (conv(("L", 3, 1)), aside(Forward, TILE["L", 3, 1], 2, 1, False)),
        ("L", 2): (conv(("E", 3)), []),
        ("E", 3): ([], []),
    }
    for k in range(4):
        last = k == 3

        def solved(h, value, k=k, last=last):
            yfull[k, h] = value
            if last:
                gather_start(Backward, 0, h, value)
            else:
                gather_start(Forward, (2 * k + 1) % 2, h, value)

        step(Forward, 2 * k, TILE["E", k], 0, None, solved, *fill["E", k])
        hand_over(yfull, ybuf, k, k).start()
        if not last:

            def reduced(h, value, k=k):
                gather_start(Forward, (2 * k + 2) % 2, h, kx[k + 1, h] - value)

            slot = None if k == 0 else k - 1
            step(Forward, 2 * k + 1, TILE["L", k + 1, k], 1 + k, slot, reduced, *fill["L", k])

    fill = {
        ("E", 3): ([], []),
        ("L", 3): (aside(Backward, TILE["L", 3, 1], 1, 1, True), aside(Backward, TILE["L", 3, 0], 1, 0, True)),
        ("E", 2): ([], []),
        ("L", 2): (aside(Backward, TILE["L", 2, 0], 2, 0, False), []),
        ("E", 1): ([], []),
        ("L", 1): ([], []),
        ("E", 0): ([], []),
    }
    t = 0
    for k in range(3, -1, -1):

        def solved(h, value, k=k, t=t):
            xfull[k, h] = value
            if k > 0:
                gather_start(Backward, (t + 1) % 2, h, value)

        step(Backward, t, TILE["E", k], 0, None, solved, *fill["E", k])
        hand_over(xfull, xbuf, k, 4 + k).start()
        if k > 0:

            def reduced(h, value, k=k, t=t):
                gather_start(Backward, (t + 2) % 2, h, yfull[k - 1, h] - value)

            slot = None if k == 3 else k - 1
            step(Backward, t + 1, TILE["L", k, k - 1], 4 - k, slot, reduced, *fill["L", k])
            t += 2

    for k in range(4):
        hand_over(yfull, ybuf, k, k).wait()
        y_ref[k, c] = yfull[k, c]
        y_ref[k, 1 - c] = ybuf[k]
    for k in range(3, -1, -1):
        hand_over(xfull, xbuf, k, 4 + k).wait()
        x_ref[k, c] = xfull[k, c]
        x_ref[k, 1 - c] = xbuf[k]


def local(k_star, lower_blocks, diag_inverse):
    steps, _, piece, cols = k_star.shape
    pairs, segments, _, width = lower_blocks.shape
    dma = pltpu.SemaphoreType.DMA
    n = len(TILES)
    pieces = pltpu.VMEM((steps, 2, piece, cols // 2), F32)
    half = pltpu.VMEM((steps, piece, cols // 2), F32)
    slots = pltpu.VMEM((2, 2, 8, piece, cols // 2), F32)
    y, x = pl.pallas_call(
        kernel,
        out_shape=[jax.ShapeDtypeStruct((steps, 2, piece, cols // 2), F32)] * 2,
        in_specs=[
            pl.BlockSpec(memory_space=pltpu.VMEM),
            pl.BlockSpec(memory_space=pl.ANY),
            pl.BlockSpec(memory_space=pl.ANY),
        ],
        out_specs=[pl.BlockSpec(memory_space=pltpu.VMEM)] * 2,
        scratch_shapes=[
            pltpu.VMEM((SLOTS, 2, 8, piece, width), F32),
            pltpu.VMEM((n, 2, 2, 512, width), BF16),
            pltpu.VMEM((n, 2, 2, 512, width), BF16),
            slots,
            slots,
            pltpu.VMEM((4, 2, 512, 256), BF16),
            slots, slots,
            slots, slots,
            half, half,
            pieces, pieces, pieces,
            half, half,
            dma((SLOTS,)), dma((SLOTS,)), dma((SLOTS,)),
            pltpu.SemaphoreType.REGULAR,
            dma((9,)), dma((9,)),
            dma((2, 2)), dma((2, 2)),
            dma((2, 2)), dma((2, 2)),
            dma((2, 2)), dma((2, 2)),
            dma((2, 2)), dma((2, 2)),
        ],
        compiler_params=pltpu.CompilerParams(
            collective_id=0, has_side_effects=True, vmem_limit_bytes=62 * 1024 * 1024
        ),
    )(
        k_star.reshape(steps, piece, cols),
        lower_blocks.reshape(pairs, segments // 2, 2, piece, width),
        diag_inverse.reshape(steps, segments // 2, 2, piece, width),
    )

    def whole(value):
        return value.transpose(0, 2, 1, 3).reshape(steps, 1, piece, cols)

    return whole(y), whole(x)


def solution(mesh):
    return jax.shard_map(
        local,
        mesh=mesh,
        in_specs=(
            P(None, "pcol", "prow", None),
            P(None, None, "prow", "pcol"),
            P(None, None, "prow", "pcol"),
        ),
        out_specs=(P(None, "pcol", "prow", None), P(None, "pcol", "prow", None)),
        check_vma=False,
    )
```

time: 1360 us -> 220 us (0.16)
  waiting for transfers between devices: 1050 us -> 0 us
  Pallas kernels: 0 us -> 215 us
  blocking collectives: 166 us -> 0 us
  matrix products: 83.7 us -> 0 us
  local copies, waits for them, and re-layouts: 23.6 us -> 4.13 us
  between operations: 14.8 us -> 0.64 us
    reduce_scatter x13 -> x0, waiting for transfers between devices: 668 us -> none  [the longest x7 480 us: sum_columns(): lax.psum_scatter(term(jnp.int32(0), piece * lax.axis_size('pcol')), 'pcol...]
    all_gather x7 -> x0, waiting for transfers between devices: 353 us -> none  [the longest x4 200 us: apply_inverse_transposed(): lax.all_gather(reduced, 'pcol', axis=0, tiled=True)]
    pallas_call x0 -> x1, Pallas kernels: none -> 215 us  [local(): pl.pallas_call(kernel, out_shape=[jax.ShapeDtypeStruct((steps, 2, piece,...]
    all_gather x7 -> x0, blocking collectives: 166 us -> none  [the longest x4 95.2 us: apply_inverse(): lax.all_gather(reduced, 'prow', axis=0, tiled=True)]
    dot_general x20 -> x0, matrix products: 83.7 us -> none  [the longest x10 44.8 us: product_left(): lax.dot_general(left, right, (((0,), (0,)), ((), ())), precision=lax.Prec...]
    unnamed x22 -> x0, waiting for transfers between devices: 30.7 us -> none
    slice x4 -> x0, local copies, waits for them, and re-layouts: 16.4 us -> none  [the longest x1 9.47 us: term(): rows = lower[pair_index(block, other)]]
  transfers between devices with their start and end apart: 21 -> 0, of which waited for: 21 -> 0; matrix products, arithmetic and copies ran while one was open for 2% -> 0% of each run, Pallas kernels for 0% -> 0%
where the time goes in v2:
time: 220 us
  Pallas kernels  215 us (98%)
  local copies, waits for them, and re-layouts  4.13 us (2%)
    pallas_call x1, Pallas kernels, local(): pl.pallas_call(kernel, out_shape=[jax.ShapeDtypeStruct((steps, 2, piece,...  215 us

profile of v2, /device:TPU:1, one launch (start us, length us, event | category | flops | bytes accessed | tf_op | source)
XLA Modules:
  0.0 219.6 jit_solution(7769647567482028139)
XLA Ops:
  0.6 214.8 %shard_map.50 = (f32[4,2,64,128]{3,2,1,0:T(8,128)}, f32[4,2,64,128]{3,2,1,0:T(8,128)}) custom-call(f32[4,64,256]{2,1,0:T(8,128)} %bitcast.13, f32[6,8,2,64,512]{4,3,2,1,0:T(8,128)} %bitcast.7, f32[4,8,2,64,512]{4,3,2,1,0:T(8,128)} %bitcast.8), custom_call_target="tpu_custom_call" | custom-call | tf_op jit(solution)/shard_map/pallas_call | solution.py:301
  215.4 1.2 copy.5
  216.6 0.9 reshape.22
  217.5 1.2 copy.6
  218.6 0.9 reshape.23

commit v3 on v2

v3 whole, which is shorter than its diff:
```python
import jax
import jax.numpy as jnp
from jax import lax
from jax.experimental import pallas as pl
from jax.experimental.pallas import tpu as pltpu
from jax.sharding import PartitionSpec as P

MESH = pl.DeviceIdType.MESH
F32 = jnp.float32
BF16 = jnp.bfloat16

SLOTS = 4
CHUNK = 256
TILES = [
    ("E", 0), ("L", 1, 0), ("E", 1), ("L", 2, 1), ("L", 2, 0),
    ("L", 3, 0), ("E", 2), ("L", 3, 2), ("L", 3, 1), ("E", 3),
]
TILE = {name: index for index, name in enumerate(TILES)}
HALVES = 2 * len(TILES)
FAR_FIRST = [(1, 2), (1, 1), (1, 3), (0, 2), (1, 0), (0, 1), (0, 3)]
ALL = [(a, b) for b in (2, 1, 3, 0) for a in (0, 1)]


def dot(a, b):
    return lax.dot_general(a, b, (((1,), (0,)), ((), ())), preferred_element_type=F32)


def dot_t(a, b):
    return lax.dot_general(a, b, (((0,), (0,)), ((), ())), preferred_element_type=F32)


def split(value):
    high = value.astype(BF16)
    return high, (value - high.astype(F32)).astype(BF16)


def kernel(
    k_ref, l_ref, e_ref, y_ref, x_ref,
    stage, mh, ml, part, acc, ops, gf, gb, rf, rb, hold, ksend, kx, yfull, xfull, ybuf, xbuf,
    ld_sem, mate_s, mate_r, free, k_s, k_r, k0_s, k0_r, y_s, y_r, x_s, x_r,
    rs_s, rs_r, ag_s, ag_r, brs_s, brs_r, bag_s, bag_r,
):
    r = lax.axis_index("prow")
    p = lax.axis_index("pcol")
    c = lax.rem(p, 2)
    q = p // 2
    mate = (r, p + 1 - 2 * c)

    def across(row):
        return lax.rem(row + 4, 8)

    turned = across(r)

    def member(me, offset):
        return lax.rem(me // 4 + offset[0], 2) * 4 + lax.rem(lax.rem(me, 4) + offset[1], 4)

    def remote(src, dst, send, recv, device):
        return pltpu.make_async_remote_copy(
            src_ref=src, dst_ref=dst, send_sem=send, recv_sem=recv, device_id=device, device_id_type=MESH
        )

    def several(buf, send, recv, count):
        view = buf.at[pl.ds(0, count)]
        return remote(view, view, send, recv, mate)

    def source(n):
        name, half = TILES[n // 2], n % 2
        if name[0] == "E":
            return e_ref.at[name[1], :, half]
        return l_ref.at[name[1] * (name[1] - 1) // 2 + name[2], :, half]

    def own(n):
        s = n % SLOTS
        return pltpu.make_async_copy(source(n), stage.at[s, c], ld_sem.at[s])

    def shared(n):
        s = n % SLOTS
        return remote(source(n), stage.at[s, c], mate_s.at[s], mate_r.at[s], mate)

    def convert(n):
        s = n % SLOTS
        own(n).wait()
        shared(n).wait()
        for kh in range(2):

            @pl.loop(0, 8)
            def _(a):
                high, low = split(stage[s, kh, a])
                rows = pl.ds(pl.multiple_of(a * 64, 64), 64)
                mh[n // 2, kh, n % 2, rows, :] = high
                ml[n // 2, kh, n % 2, rows, :] = low

        if n + SLOTS < HALVES:
            pl.semaphore_signal(free, inc=1, device_id=mate, device_id_type=MESH)
        following = n - 1 + SLOTS
        if n >= 1 and following < HALVES:
            pl.semaphore_wait(free, 1)
            own(following).start()
            shared(following).start()

    for n in range(SLOTS):
        own(n).start()
    for k in range(4):
        ksend[0, k] = k_ref[k, :, 0:128]
        ksend[1, k] = k_ref[k, :, 128:256]
    gf[0, c, r] = jnp.where(c == 0, k_ref[0, :, 0:128], k_ref[0, :, 128:256])
    for h in range(2):
        rf[0, h] = jnp.zeros((8, 64, 128), F32)
        gb[0, h] = jnp.zeros((8, 64, 128), F32)

    barrier = pltpu.get_barrier_semaphore()

    def greet(device):
        pl.semaphore_signal(barrier, inc=1, device_id=device, device_id_type=MESH)

    greet(mate)
    for offset in FAR_FIRST:
        greet((member(r, offset), p))
        greet((member(r, offset), mate[1]))
        greet((turned, 2 * member(q, offset) + c))
    pl.semaphore_wait(barrier, 22)

    def first(offset, same):
        row = member(r, offset)
        half = c if same else 1 - c
        return remote(
            ksend.at[half, 0], gf.at[0, c, r], k0_s.at[0 if same else 1], k0_r.at[0 if same else 1],
            (row, p if same else mate[1]),
        )

    for offset in FAR_FIRST:
        first(offset, True).start()
        first(offset, False).start()
    first((0, 0), False).start()
    for n in range(SLOTS):
        shared(n).start()

    def later(core):
        return remote(ksend.at[core], kx.at[c], k_s.at[core], k_r.at[c], (turned, 2 * q + core))

    def arrived(core):
        return remote(ksend.at[core], kx.at[core], k_s.at[core], k_r.at[core], mate)

    for core in range(2):
        later(core).start()

    class Forward:
        @staticmethod
        def product(i, kh, oh, b, at):
            rows = pl.ds(at, CHUNK)
            wide = dot(mh[i, kh, oh, rows, :], ops[b, kh])
            return wide[:, 0:128] + wide[:, 128:256] + dot(ml[i, kh, oh, rows, :], ops[b, kh, :, 0:128])

    class Backward:
        @staticmethod
        def product(i, kh, oh, b, at):
            cols = pl.ds(at, CHUNK)
            wide = dot_t(mh[i, oh, kh, :, cols], ops[b, kh])
            return wide[:, 0:128] + wide[:, 128:256] + dot_t(ml[i, oh, kh, :, cols], ops[b, kh, :, 0:128])

    PER = CHUNK // 64

    def chunks():
        return range(0, 512, CHUNK)

    def groups(value):
        return value.reshape(PER, 64, 128)

    def over_columns(n, needed, message):
        for j, offset in enumerate(ALL):
            other = member(q, offset)
            if n > 0:
                message(j, other)
            else:
                pl.when(needed(other))(lambda j=j, other=other: message(j, other))

    def from_columns(n, needed, message):
        for j, offset in enumerate(ALL):
            other = member(q, (offset[0], (4 - offset[1]) % 4))
            if n > 0:
                message(j, other)
            else:
                pl.when(needed(other))(lambda j=j, other=other: message(j, other))

    def below(other):
        return other >= q

    def above(other):
        return other <= q

    def fwd_gather_start(par, h, value):
        gf[par, h, turned] = value
        for offset in FAR_FIRST:
            remote(
                gf.at[par, h, turned], gf.at[par, h, turned], ag_s.at[par, h], ag_r.at[par, h],
                (member(r, offset), p),
            ).start()

    def fwd_gather_wait(n, h):
        par = min(n, 1)
        several(gf.at[par, h], ag_s.at[par, h], ag_r.at[par, h], 7).wait_recv()

    def fwd_gather_sent(n, h):
        par = min(n, 1)
        several(gf.at[par, h], ag_s.at[par, h], ag_r.at[par, h], 7).wait_send()

    def fwd_message(n, h):
        def make(j, other):
            return remote(
                part.at[min(n, 1), h, other], rf.at[n, h, j], rs_s.at[n, h, j], rs_r.at[n, h, j],
                (turned, 2 * other + c),
            )

        return make

    def fwd_sum_start(n, h, natural):
        over_columns(n, below, lambda j, other: fwd_message(n, h)(j, other).start())

    def fwd_sum_finish(n, h, natural):
        from_columns(n, above, lambda j, other: fwd_message(n, h)(j, other).wait_recv())
        total = rf[n, h, 0]
        for j in range(1, 8):
            total = total + rf[n, h, j]
        return total

    def fwd_sum_sent(n, h):
        over_columns(n, below, lambda j, other: fwd_message(n, h)(j, other).wait_send())

    def bwd_message(n, h):
        def make(j, other):
            return remote(
                hold.at[min(n, 1), h], gb.at[n, h, q], bag_s.at[n, h, j], bag_r.at[n, h, j],
                (turned, 2 * other + c),
            )

        return make

    def bwd_gather_start(n, h, value):
        hold[min(n, 1), h] = value
        over_columns(n, above, lambda j, other: bwd_message(n, h)(j, other).start())

    def bwd_gather_wait(n, h):
        def wait(j, other):
            slot = gb.at[n, h, other]
            remote(slot, slot, bag_s.at[n, h, j], bag_r.at[n, h, j], mate).wait_recv()

        from_columns(n, below, wait)

    def bwd_gather_sent(n, h):
        over_columns(n, above, lambda j, other: bwd_message(n, h)(j, other).wait_send())

    def bwd_sum_start(n, h, natural):
        par = min(n, 1)
        for j, offset in enumerate(FAR_FIRST):
            other = member(r, offset)
            remote(
                part.at[par, h, other if natural else across(other)], rb.at[par, h, j],
                brs_s.at[par, h], brs_r.at[par, h], (other, p),
            ).start()

    def bwd_sum_finish(n, h, natural):
        par = min(n, 1)
        total = part[par, h, r if natural else turned]
        several(rb.at[par, h], brs_s.at[par, h], brs_r.at[par, h], 7).wait_recv()
        for j in range(7):
            total = total + rb[par, h, j]
        return total

    def bwd_sum_sent(n, h):
        par = min(n, 1)
        several(rb.at[par, h], brs_s.at[par, h], brs_r.at[par, h], 7).wait_send()

    Forward.g, Forward.gather_wait, Forward.gather_sent = gf, staticmethod(fwd_gather_wait), staticmethod(fwd_gather_sent)
    Forward.sum_start, Forward.sum_finish = staticmethod(fwd_sum_start), staticmethod(fwd_sum_finish)
    Forward.sum_sent = staticmethod(fwd_sum_sent)
    Backward.g, Backward.gather_wait, Backward.gather_sent = gb, staticmethod(bwd_gather_wait), staticmethod(bwd_gather_sent)
    Backward.sum_start, Backward.sum_finish = staticmethod(bwd_sum_start), staticmethod(bwd_sum_finish)
    Backward.sum_sent = staticmethod(bwd_sum_sent)

    def take(way, n, h, b):
        high, low = split(way.g[n if way is Backward else min(n, 1), h].reshape(512, 128))
        ops[b, h, :, 0:128] = high
        ops[b, h, :, 128:256] = low

    def aside(way, i, b, slot, first):
        def run(oh):
            for at in chunks():
                out = way.product(i, 0, oh, b, at) + way.product(i, 1, oh, b, at)
                where = pl.ds(at // 64, PER)
                out = groups(out)
                acc[slot, oh, where] = out if first else acc[slot, oh, where] + out

        return [lambda oh=oh: run(oh) for oh in range(2)]

    def step(way, n, i, b, slot, after, summing, gathering, opening=False, natural=False):
        par = min(n, 1)
        if not opening:
            way.gather_wait(n, 0)
        take(way, n, 0, b)
        for oh in range(2):
            for at in chunks():
                where = pl.ds(at // 64, PER)
                out = groups(way.product(i, 0, oh, b, at))
                part[par, oh, where] = out if slot is None else out + acc[slot, oh, where]
        if not opening:
            way.gather_wait(n, 1)
        take(way, n, 1, b)
        for oh in range(2):
            for at in chunks():
                where = pl.ds(at // 64, PER)
                part[par, oh, where] = part[par, oh, where] + groups(way.product(i, 1, oh, b, at))
            way.sum_start(n, oh, natural)
        if not opening:
            for h in range(2):
                way.gather_sent(n, h)
        for run in summing:
            run()
        for h in range(2):
            after(h, way.sum_finish(n, h, natural))
        for run in gathering:
            run()
        for h in range(2):
            way.sum_sent(n, h)

    def hand_over(full, buf, k, sems, pp):
        return remote(
            full.at[k, pp], buf.at[k, c], sems[0].at[k, pp], sems[1].at[k, c], (turned, 2 * q + pp)
        )

    def handed_over(full, buf, k, sems, core):
        remote(full.at[k, core], buf.at[k, core], sems[0].at[k, core], sems[1].at[k, core], mate).wait()

    def conv(*names):
        return [lambda n=n: convert(n) for name in names for n in (2 * TILE[name], 2 * TILE[name] + 1)]

    for run in conv(("E", 0)):
        run()
    several(gf.at[0, c], k0_s.at[0], k0_r.at[0], 7).wait()
    several(gf.at[0, 1 - c], k0_s.at[1], k0_r.at[1], 8).wait()
    fill = {
        ("E", 0): (conv(("L", 1, 0)), conv(("E", 1))),
        ("L", 0): (conv(("L", 2, 1)), conv(("L", 2, 0))),
        ("E", 1): (aside(Forward, TILE["L", 2, 0], 1, 0, True), conv(("L", 3, 0))),
        ("L", 1): (conv(("E", 2)), aside(Forward, TILE["L", 3, 0], 1, 1, True) + conv(("L", 3, 2))),
        ("E", 2): (conv(("L", 3, 1)), aside(Forward, TILE["L", 3, 1], 2, 1, False)),
        ("L", 2): (conv(("E", 3)), []),
        ("E", 3): ([], []),
    }
    for k in range(4):
        last = k == 3

        def solved(h, value, k=k, last=last):
            yfull[k, h] = value
            if last:
                bwd_gather_start(0, h, value)
            else:
                fwd_gather_start(1, h, value)

        step(Forward, 0, TILE["E", k], 0, None, solved, *fill["E", k], opening=k == 0)
        for pp in range(2):
            hand_over(yfull, ybuf, k, (y_s, y_r), pp).start()
        if not last:
            if k == 0:
                for core in range(2):
                    arrived(core).wait()

            def reduced(h, value, k=k):
                fwd_gather_start(0, h, kx[h, k + 1] - value)

            slot = None if k == 0 else k - 1
            step(Forward, 1 + k, TILE["L", k + 1, k], 1 + k, slot, reduced, *fill["L", k])

    fill = {
        ("E", 3): ([], []),
        ("L", 3): (aside(Backward, TILE["L", 3, 1], 1, 1, True), aside(Backward, TILE["L", 3, 0], 1, 0, True)),
        ("E", 2): ([], []),
        ("L", 2): (aside(Backward, TILE["L", 2, 0], 2, 0, False), []),
        ("E", 1): ([], []),
        ("L", 1): ([], []),
        ("E", 0): ([], []),
    }
    for k in range(3, -1, -1):

        def solved(h, value, k=k):
            xfull[k, h] = value
            if k > 0:
                bwd_gather_start(4 - k, h, value)

        step(Backward, 0, TILE["E", k], 0, None, solved, *fill["E", k], natural=k == 0)
        if k > 0:
            for pp in range(2):
                hand_over(xfull, xbuf, k, (x_s, x_r), pp).start()

            def reduced(h, value, k=k):
                bwd_gather_start(0, h, yfull[k - 1, h] - value)

            slot = None if k == 3 else k - 1
            step(Backward, 4 - k, TILE["L", k, k - 1], 4 - k, slot, reduced, *fill["L", k])

    final = remote(xfull.at[0, 1 - c], xbuf.at[0, c], x_s.at[0, 0], x_r.at[0, 0], mate)
    final.start()
    xbuf[0, c] = xfull[0, c]
    for k in range(4):
        for core in range(2):
            handed_over(yfull, ybuf, k, (y_s, y_r), core)
            y_ref[k, :, 128 * core : 128 * core + 128] = ybuf[k, core]
    for k in range(3, -1, -1):
        if k == 0:
            final.wait()
        for core in range(2):
            if k > 0:
                handed_over(xfull, xbuf, k, (x_s, x_r), core)
            x_ref[k, :, 128 * core : 128 * core + 128] = xbuf[k, core]


def local(k_star, lower_blocks, diag_inverse):
    steps, _, piece, cols = k_star.shape
    pairs, segments, _, width = lower_blocks.shape
    dma = pltpu.SemaphoreType.DMA
    n = len(TILES)
    pieces = pltpu.VMEM((steps, 2, piece, cols // 2), F32)
    halves = pltpu.VMEM((2, steps, piece, cols // 2), F32)
    slots = pltpu.VMEM((2, 2, 8, piece, cols // 2), F32)
    more = pltpu.VMEM((4, 2, 8, piece, cols // 2), F32)
    y, x = pl.pallas_call(
        kernel,
        out_shape=[jax.ShapeDtypeStruct((steps, piece, cols), F32)] * 2,
        in_specs=[
            pl.BlockSpec(memory_space=pltpu.VMEM),
            pl.BlockSpec(memory_space=pl.ANY),
            pl.BlockSpec(memory_space=pl.ANY),
        ],
        out_specs=[pl.BlockSpec(memory_space=pltpu.VMEM)] * 2,
        scratch_shapes=[
            pltpu.VMEM((SLOTS, 2, 8, piece, width), F32),
            pltpu.VMEM((n, 2, 2, 512, width), BF16),
            pltpu.VMEM((n, 2, 2, 512, width), BF16),
            slots,
            slots,
            pltpu.VMEM((4, 2, 512, 256), BF16),
            slots, more,
            more, slots,
            pltpu.VMEM((2, 2, piece, cols // 2), F32),
            halves, halves,
            pieces, pieces, pieces, pieces,
            dma((SLOTS,)), dma((SLOTS,)), dma((SLOTS,)),
            pltpu.SemaphoreType.REGULAR,
            dma((2,)), dma((2,)), dma((2,)), dma((2,)),
            dma((4, 2)), dma((4, 2)), dma((4, 2)), dma((4, 2)),
            dma((4, 2, 8)), dma((4, 2, 8)),
            dma((2, 2)), dma((2, 2)),
            dma((2, 2)), dma((2, 2)),
            dma((4, 2, 8)), dma((4, 2, 8)),
        ],
        compiler_params=pltpu.CompilerParams(
            collective_id=0, has_side_effects=True, vmem_limit_bytes=62 * 1024 * 1024
        ),
    )(
        k_star.reshape(steps, piece, cols),
        lower_blocks.reshape(pairs, segments // 2, 2, piece, width),
        diag_inverse.reshape(steps, segments // 2, 2, piece, width),
    )

    shape = (steps, 1, piece, cols)
    return y.reshape(shape), x.reshape(shape)


def solution(mesh):
    return jax.shard_map(
        local,
        mesh=mesh,
        in_specs=(
            P(None, "pcol", "prow", None),
            P(None, None, "prow", "pcol"),
            P(None, None, "prow", "pcol"),
        ),
        out_specs=(P(None, "pcol", "prow", None), P(None, "pcol", "prow", None)),
        check_vma=False,
    )
```

time: 220 us -> 213 us (0.968)
  Pallas kernels: 215 us -> 209 us
    pallas_call x1, Pallas kernels: 215 us -> 209 us  [local(): pl.pallas_call(kernel, out_shape=[jax.ShapeDtypeStruct((steps, piece, col...]
    unnamed x0 -> x2, local copies, waits for them, and re-layouts: none -> 3.35 us
    transpose x2 -> x0, local copies, waits for them, and re-layouts: 2.31 us -> none  [whole(): return value.transpose(0, 2, 1, 3).reshape(steps, 1, piece, cols)]
where the time goes in v3:
time: 213 us
  Pallas kernels  209 us (98%)
  local copies, waits for them, and re-layouts  3.35 us (2%)
    pallas_call x1, Pallas kernels, local(): pl.pallas_call(kernel, out_shape=[jax.ShapeDtypeStruct((steps, piece, col...  209 us

profile of v3, /device:TPU:1, one launch (start us, length us, event | category | flops | bytes accessed | tf_op | source)
XLA Modules:
  0.0 213.2 jit_solution(909603411796017430)
XLA Ops:
  0.6 209.2 %shard_map.50 = (f32[4,64,256]{2,1,0:T(8,128)}, f32[4,64,256]{2,1,0:T(8,128)}) custom-call(f32[4,64,256]{2,1,0:T(8,128)} %bitcast.13, f32[6,8,2,64,512]{4,3,2,1,0:T(8,128)} %bitcast.9, f32[4,8,2,64,512]{4,3,2,1,0:T(8,128)} %bitcast.10), custom_call_target="tpu_custom_call" | custom-call | tf_op jit(solution)/shard_map/pallas_call | solution.py:425
  209.9 1.7 copy.9
  211.5 1.7 copy.10

commit v4 on v3

--- a/solution.py
+++ b/solution.py
@@ -10,7 +10,7 @@
 BF16 = jnp.bfloat16
 
 SLOTS = 4
-CHUNK = 256
+CHUNK = 512
 TILES = [
     ("E", 0), ("L", 1, 0), ("E", 1), ("L", 2, 1), ("L", 2, 0),
     ("L", 3, 0), ("E", 2), ("L", 3, 2), ("L", 3, 1), ("E", 3),
@@ -52,7 +52,7 @@
     turned = across(r)
 
     def member(me, offset):
-        return lax.rem(me // 4 + offset[0], 2) * 4 + lax.rem(lax.rem(me, 4) + offset[1], 4)
+        return lax.rem(me // 4 + offset[0], 2) * 4 + lax.rem(lax.rem(me, 4) + offset[1] * (1 + 2 * c), 4)
 
     def remote(src, dst, send, recv, device):
         return pltpu.make_async_remote_copy(

time: 213 us -> 213 us (level)
  no operation moved by 1% of the time
where the time goes in v4:
time: 213 us; the launch traced here: 212 us
  Pallas kernels  208 us (98%)
  local copies, waits for them, and re-layouts  3.35 us (2%)
    pallas_call x1, Pallas kernels, local(): pl.pallas_call(kernel, out_shape=[jax.ShapeDtypeStruct((steps, piece, col...  208 us

profile of v4, /device:TPU:1, one launch (start us, length us, event | category | flops | bytes accessed | tf_op | source)
XLA Modules:
  0.0 212.5 jit_solution(1533535134035019625)
XLA Ops:
  0.6 208.5 %shard_map.50 = (f32[4,64,256]{2,1,0:T(8,128)}, f32[4,64,256]{2,1,0:T(8,128)}) custom-call(f32[4,64,256]{2,1,0:T(8,128)} %bitcast.13, f32[6,8,2,64,512]{4,3,2,1,0:T(8,128)} %bitcast.9, f32[4,8,2,64,512]{4,3,2,1,0:T(8,128)} %bitcast.10), custom_call_target="tpu_custom_call" | custom-call | tf_op jit(solution)/shard_map/pallas_call | solution.py:425
  209.1 1.7 copy.9
  210.8 1.7 copy.10
